TPU v7x, 32 devices: a whole 2x2x4 slice. The times are simulated.
32 devices in a mesh: chan: 8 (over z, y), grp: 4 (over x, core).
Axes of the slice: x: 2, y: 2, z: 4, core: 2. Of those that a mesh axis runs over, the one named last changes fastest.
Arguments:
- beam_power: bfloat16 [32, 8192, 128], P('grp', 'chan'), as said below
- trial_blocks: int32 [32], replicated, may hold values from 1 to 4, as said below
- shift_table: int32 [4, 5, 8192], replicated, may hold values from 0 to 4, as said below
Outputs:
- dm_planes: bfloat16 [32, 4, 8192, 128], P(('grp', 'chan'))
Inputs may be any that keep to these rules, and one draw needn't show every extreme that they name: `beam_power`: detected power, drawn afresh for every beam, channel and sample. `trial_blocks`: DM blocks needed by each beam. `shift_table`: delays in whole tiles.
All inputs are finite; a program needn't handle non-finite values.
Results may differ from a plain program's by a relative error of at most 0.0049.
Values may be sent and summed in bfloat16 or wider, within the bound.
A program may use at most 128 MiB of HBM per device.

v0:
```python
import functools

import jax
import jax.numpy as jnp
from jax import lax
from jax.experimental import pallas as pl
from jax.experimental.pallas import tpu as pltpu
from jax.sharding import PartitionSpec as P

SECTIONS = 5
MAXBLK = 4
TILE = 8
BAND = 2**SECTIONS
LANES = 128
MESH = pl.DeviceIdType.MESH

epsilon = 1e-05
out_scale = float(2**SECTIONS) ** (-0.5)


def flip(me, k):
    out = me
    bit = 1
    while bit <= k:
        if k & bit:
            out = out + bit * (1 - 2 * ((me // bit) % 2))
        bit *= 2
    return out


def eye(size):
    r = lax.broadcasted_iota(jnp.int32, (size, size), 0)
    c = lax.broadcasted_iota(jnp.int32, (size, size), 1)
    return (r == c).astype(jnp.float32).astype(jnp.bfloat16)


def times_transposed(a, b):
    return lax.dot_general(a, b, (((1,), (1,)), ((), ())), preferred_element_type=jnp.float32)


def bands_to_lanes(ident, x_ref, d, first):
    sources, _, bands, time_len = x_ref.shape
    if bands % 16 == 0:
        part = jnp.concatenate([x_ref[i, d] for i in range(sources)], axis=0)
    else:
        part = jnp.concatenate([x_ref[i, d].astype(jnp.float32) for i in range(sources)], axis=0)
        part = part.astype(jnp.bfloat16)
    turned = times_transposed(ident, part)
    if sources * bands < LANES:
        turned = jnp.concatenate([turned[: time_len // 2], turned[time_len // 2 :]], axis=1)
    first[d] = turned.reshape(first.shape[1:])


def merge_row(source, low_row, up_row, amount, split):
    tiles = source.shape[1]
    odd = (amount == 1) | (amount == 3)
    two = (amount == 2) | (amount == 3)
    four = amount == 4
    zero = jnp.zeros((TILE, LANES), jnp.float32)
    ups = {t: source[up_row, t] for t in range(tiles)}
    if split:
        late = lax.broadcasted_iota(jnp.int32, (TILE, LANES), 1) >= LANES // 2
        for t in range(-4, 0):
            ups[t] = jnp.where(late, pltpu.roll(ups[tiles + t], LANES // 2, 1), zero)
    ones, out = {}, []
    for t in range(-2 if split else 0, tiles):
        ones[t] = jnp.where(odd, ups.get(t - 1, zero), ups[t])
    for t in range(tiles):
        value = jnp.where(two, ones.get(t - 2, zero), ones[t])
        value = jnp.where(four, ups.get(t - 4, zero), value)
        out.append(source[low_row, t] + value)
    return out


def merge_pair(s, p, source, target, table_row, ident, stage, split):
    half = 2**s
    base = (p // half) * (2 * half)
    j = p % half
    if isinstance(p, int):
        after = min(j + 1, half - 1)
    else:
        after = jnp.minimum(j + 1, half - 1)
    rows = []
    for odd, up in ((0, j), (1, after)):
        amount = jnp.broadcast_to(table_row(s, 2 * p + odd), (TILE, LANES))
        rows.append(merge_row(source, base + j, base + half + up, amount, split))
    if s < SECTIONS - 1:
        for odd in range(2):
            for t, value in enumerate(rows[odd]):
                target[2 * p + odd, t] = value
        return
    time_len = len(rows[0]) * TILE
    both = [(value * out_scale) for row in rows for value in row]
    both = jnp.concatenate(both, axis=0).astype(jnp.bfloat16)
    turned = times_transposed(ident, both)
    bands = LANES // 2 if split else LANES
    for odd in range(2):
        row = turned[:, odd * time_len : (odd + 1) * time_len]
        if split:
            row = jnp.concatenate([row[:bands], row[bands:]], axis=1)
        stage[pl.ds(2 * p + odd, bands, stride=BAND), :] = row


def sections_loop(first, buf_a, buf_b, stage, table_row, ident, split):
    source = first
    for s in range(SECTIONS):
        target = (buf_a, buf_b)[s % 2]

        def step(p, inner, s=s, source=source, target=target):
            merge_pair(s, p, source, target, table_row, ident, stage, split)
            return inner

        lax.fori_loop(0, BAND // 2, step, 0)
        source = target


def turn_kernel(
    n, bands, time_len,
    power_hbm, table_hbm,
    near_out, mid_out, far_ref, far_table,
    power, table, rows, packed, near, mid, lines, tab_near, tab_mid, tab_far,
    first, buf_a, buf_b, stage, first_q, buf_aq, buf_bq, stage_q, planes, planes_q,
    in_sem, table_sem, send_sem, recv_sem, own_sem, out_sem, out_sem_q, tab_sem,
):
    me = lax.axis_index("chan")
    grp = lax.axis_index("grp")
    half = n // 2
    quarter = n // 4
    order = list(range(half, half + quarter)) + list(range(half - 1, -1, -1)) + list(range(half + quarter, n))

    loads = {}
    for k in order:
        loads[k] = pltpu.make_async_copy(power_hbm.at[flip(me, k)], power.at[k], in_sem.at[k])
        loads[k].start()
    table_load = pltpu.make_async_copy(table_hbm, table, table_sem)
    table_load.start()

    barrier = pltpu.get_barrier_semaphore()
    for k in range(1, n):
        pl.semaphore_signal(barrier, inc=1, device_id=(flip(me, k), grp), device_id_type=MESH)
    pl.semaphore_wait(barrier, n - 1)

    copies = {}
    for k in order:
        loads[k].wait()
        values = power[k].astype(jnp.float32)
        center = jnp.mean(values, axis=-1, keepdims=True)
        moved = values - center
        spread = jnp.mean(jnp.square(moved), axis=-1, keepdims=True)
        rows[...] = moved * lax.rsqrt(spread + epsilon)
        for d in range(BAND):
            packed[k, d] = rows[pl.ds(d, bands, stride=BAND), :].astype(jnp.bfloat16)
        if k < half:
            place = near.at[me % half]
        elif k < half + quarter:
            place = mid.at[me % quarter]
        else:
            place = far_ref.at[me % quarter]
        if k == 0:
            copies[k] = pltpu.make_async_copy(packed.at[k], place, own_sem)
        else:
            copies[k] = pltpu.make_async_remote_copy(
                src_ref=packed.at[k],
                dst_ref=place,
                send_sem=send_sem.at[k],
                recv_sem=recv_sem.at[k],
                device_id=(flip(me, k), grp),
                device_id_type=MESH,
            )
        copies[k].start()

    table_load.wait()
    ident = eye(LANES)
    groups = table.shape[2] // LANES
    per_group = LANES // BAND
    group_row = lax.broadcasted_iota(jnp.int32, (groups, LANES), 0)
    lane = lax.broadcasted_iota(jnp.int32, (groups, LANES), 1)
    lane_q = lane % (LANES // 2)
    parts = (
        ((me // half) * LANES, lane, tab_near),
        ((flip(me, half) // quarter) * (LANES // 2), lane_q, tab_mid),
        ((flip(me, half + quarter) // quarter) * (LANES // 2), lane_q, tab_far),
    )

    def order_table(s, carry):
        for c in range(groups):
            lines[pl.ds(c, MAXBLK, stride=groups), :] = table[s, :, c * LANES : (c + 1) * LANES].astype(
                jnp.float32
            )
        for block in range(MAXBLK):
            part = lines[block * groups : (block + 1) * groups, :].astype(jnp.bfloat16)
            turned = times_transposed(ident, part).astype(jnp.bfloat16)
            for start, lanes, target in parts:
                total = jnp.zeros((BAND, LANES), jnp.float32)
                for b in range(per_group):
                    place = (group_row * per_group + b) - start == lanes
                    place = place.astype(jnp.float32).astype(jnp.bfloat16)
                    total += jnp.dot(
                        turned[b * BAND : (b + 1) * BAND], place, preferred_element_type=jnp.float32
                    )
                target[block, s] = total.astype(jnp.int32)
        return carry

    lax.fori_loop(0, SECTIONS, order_table, 0)
    tab_copy = pltpu.make_async_copy(tab_far, far_table, tab_sem)
    tab_copy.start()

    copies[0].wait()
    for k in range(1, half):
        copies[k].wait_recv()

    def fill(d, carry):
        bands_to_lanes(ident, near, d, first)
        return carry

    lax.fori_loop(0, BAND, fill, 0)

    def near_block(block, carry):
        def table_row(s, row):
            return tab_near[block, s, pl.ds(row, 1), :]

        sections_loop(first, buf_a, buf_b, stage, table_row, ident, False)
        planes[block] = stage[...].astype(jnp.bfloat16)
        pltpu.make_async_copy(planes.at[block], near_out.at[block], out_sem.at[block]).start()
        return carry

    lax.fori_loop(0, MAXBLK, near_block, 0)

    for k in range(half, half + quarter):
        copies[k].wait_recv()

    def fill_q(d, carry):
        bands_to_lanes(ident, mid, d, first_q)
        return carry

    lax.fori_loop(0, BAND, fill_q, 0)

    def mid_block(block, carry):
        def table_row(s, row):
            return tab_mid[block, s, pl.ds(row, 1), :]

        sections_loop(first_q, buf_aq, buf_bq, stage_q, table_row, ident, True)
        planes_q[block] = stage_q[...].astype(jnp.bfloat16)
        pltpu.make_async_copy(planes_q.at[block], mid_out.at[block], out_sem_q.at[block]).start()
        return carry

    lax.fori_loop(0, MAXBLK, mid_block, 0)

    for block in range(MAXBLK):
        pltpu.make_async_copy(planes.at[block], near_out.at[block], out_sem.at[block]).wait()
        pltpu.make_async_copy(planes_q.at[block], mid_out.at[block], out_sem_q.at[block]).wait()
    tab_copy.wait()
    for k in range(1, n):
        copies[k].wait_send()
    for k in range(half + quarter, n):
        copies[k].wait_recv()


def turn(power, table, n):
    beams, chans, time_len = power.shape
    bands = chans // BAND
    sections, blocks, total_rows = table.shape
    half_rows = LANES * BAND
    tiles = time_len // TILE
    groups = total_rows // LANES
    any_spec = pl.BlockSpec(memory_space=pl.ANY)
    wide = pltpu.VMEM((BAND, tiles, TILE, LANES), jnp.float32)
    wide_q = pltpu.VMEM((BAND, tiles // 2, TILE, LANES), jnp.float32)
    ordered = (blocks, sections, BAND, LANES)
    return pl.pallas_call(
        functools.partial(turn_kernel, n, bands, time_len),
        out_shape=(
            jax.ShapeDtypeStruct((blocks, half_rows, time_len), jnp.bfloat16),
            jax.ShapeDtypeStruct((blocks, half_rows // 2, time_len), jnp.bfloat16),
            jax.ShapeDtypeStruct((n // 4, BAND, bands, time_len), jnp.bfloat16),
            jax.ShapeDtypeStruct(ordered, jnp.int32),
        ),
        in_specs=[any_spec, any_spec],
        out_specs=(any_spec, any_spec, any_spec, any_spec),
        scratch_shapes=[
            pltpu.VMEM((n, chans, time_len), jnp.bfloat16),
            pltpu.VMEM(table.shape, jnp.int32),
            pltpu.VMEM((chans, time_len), jnp.float32),
            pltpu.VMEM((n, BAND, bands, time_len), jnp.bfloat16),
            pltpu.VMEM((n // 2, BAND, bands, time_len), jnp.bfloat16),
            pltpu.VMEM((n // 4, BAND, bands, time_len), jnp.bfloat16),
            pltpu.VMEM((blocks * groups, LANES), jnp.float32),
            pltpu.VMEM(ordered, jnp.int32),
            pltpu.VMEM(ordered, jnp.int32),
            pltpu.VMEM(ordered, jnp.int32),
            wide,
            wide,
            wide,
            pltpu.VMEM((half_rows, time_len), jnp.float32),
            wide_q,
            wide_q,
            wide_q,
            pltpu.VMEM((half_rows // 2, time_len), jnp.float32),
            pltpu.VMEM((blocks, half_rows, time_len), jnp.bfloat16),
            pltpu.VMEM((blocks, half_rows // 2, time_len), jnp.bfloat16),
            pltpu.SemaphoreType.DMA((n,)),
            pltpu.SemaphoreType.DMA,
            pltpu.SemaphoreType.DMA((n,)),
            pltpu.SemaphoreType.DMA((n,)),
            pltpu.SemaphoreType.DMA,
            pltpu.SemaphoreType.DMA((blocks,)),
            pltpu.SemaphoreType.DMA((blocks,)),
            pltpu.SemaphoreType.DMA,
        ],
        compiler_params=pltpu.CompilerParams(
            collective_id=0, has_side_effects=True, vmem_limit_bytes=58 * 2**20
        ),
        name="turn",
    )(power, table)


def fdmt_kernel(n, count_ref, x_ref, tab_ref, near_ref, mid_ref, o_ref, first, buf_a, buf_b, stage):
    block = pl.program_id(0)
    me = lax.axis_index("chan")
    count = count_ref[lax.axis_index("grp") * n + me]
    half = n // 2
    quarter = n // 4
    quarter_rows = mid_ref.shape[1]

    def rows_of(first_quarter, size):
        start = pl.multiple_of(first_quarter * quarter_rows, quarter_rows)
        return pl.ds(start, size * quarter_rows)

    @pl.when(block == 0)
    def _():
        ident = eye(x_ref.shape[3])
        for d in range(BAND):
            bands_to_lanes(ident, x_ref, d, first)

    @pl.when(block < count)
    def _():
        ident = eye(LANES)

        def table_row(s, row):
            return tab_ref[0, s, pl.ds(row, 1), :]

        o_ref[0, 0, rows_of((me // half) * 2, 2), :] = near_ref[0]
        o_ref[0, 0, rows_of(flip(me, half) // quarter, 1), :] = mid_ref[0]
        source = first
        for s in range(SECTIONS):
            target = (buf_a, buf_b)[s % 2]
            for p in range(BAND // 2):
                merge_pair(s, p, source, target, table_row, ident, stage, True)
            source = target
        o_ref[0, 0, rows_of(flip(me, half + quarter) // quarter, 1), :] = stage[...].astype(jnp.bfloat16)

    @pl.when(block >= count)
    def _():
        o_ref[...] = jnp.zeros_like(o_ref)


def fdmt(counts, far, table, near, mid, n):
    sources, _, bands, time_len = far.shape
    blocks, half_rows, _ = near.shape
    rows = 2 * half_rows
    wide = pltpu.VMEM((BAND, time_len // TILE // 2, TILE, LANES), jnp.float32)
    return pl.pallas_call(
        functools.partial(fdmt_kernel, n),
        grid=(blocks,),
        out_shape=jax.ShapeDtypeStruct((1, blocks, rows, time_len), jnp.bfloat16),
        in_specs=[
            pl.BlockSpec(memory_space=pltpu.SMEM),
            pl.BlockSpec(far.shape, lambda j: (0, 0, 0, 0)),
            pl.BlockSpec((1,) + table.shape[1:], lambda j: (j, 0, 0, 0)),
            pl.BlockSpec((1, half_rows, time_len), lambda j: (j, 0, 0)),
            pl.BlockSpec((1, half_rows // 2, time_len), lambda j: (j, 0, 0)),
        ],
        out_specs=pl.BlockSpec((1, 1, rows, time_len), lambda j: (0, j, 0, 0)),
        scratch_shapes=[wide, wide, wide, pltpu.VMEM((half_rows // 2, time_len), jnp.float32)],
        compiler_params=pltpu.CompilerParams(vmem_limit_bytes=58 * 2**20),
        name="fdmt",
    )(counts, far, table, near, mid)


def body(beam_power, trial_blocks, shift_table):
    n = lax.axis_size("chan")
    near, mid, far, far_table = turn(beam_power, shift_table.swapaxes(0, 1), n)
    return fdmt(trial_blocks, far, far_table, near, mid, n)


def solution(mesh):
    in_specs = (P("grp", "chan", None), P(), P())
    out_specs = P(("grp", "chan"), None, None, None)
    return jax.shard_map(body, mesh=mesh, in_specs=in_specs, out_specs=out_specs, check_vma=False)
```

profile of v0, /device:TPU:0, one launch (start us, length us, event | category | flops | bytes accessed | tf_op | source)
XLA Modules:
  0.0 121.7 jit_solution(1053013511208487233)
XLA Ops:
  0.0 111.7 %turn.1 = (bf16[4,4096,128]{2,1,0:T(8,128)(2,1)}, bf16[4,2048,128]{2,1,0:T(8,128)(2,1)}, bf16[2,32,32,128]{3,2,1,0:T(8,128)(2,1)}, s32[4,5,32,128]{3,2,1,0:T(8,128)}) custom-call(bf16[8,1024,128]{2,1,0:T(8,128)(2,1)} %power_hbm.1, s32[5,4,8192]{2,1,0:T(4,128)} %bitcast.1), custom_call_target="tpu_custom_call" | custom-call | tf_op jit(solution)/shard_map/turn/pallas_call | solution.py:270
  111.7 10.0 %fdmt.1 = bf16[1,4,8192,128]{3,2,1,0:T(8,128)(2,1)} custom-call(s32[32]{0:T(128)} %count_ref.1, bf16[2,32,32,128]{3,2,1,0:T(8,128)(2,1)} %get-tuple-element.9.x_ref, s32[4,5,32,128]{3,2,1,0:T(8,128)} %get-tuple-element.10.tab_ref, bf16[4,4096,128]{2,1,0:T(8,128)(2,1)} %get-tuple-element.11.near_ref, bf16[4,2048,128]{2,1,0:T(8,128)(2,1)} %get-tuple-element.12.mid_ref), custom_call_target="tpu_custom_call" | custom-call | tf_op jit(solution)/shard_map/fdmt/pallas_call | solution.py:362
where the time goes:
time: 123 us; the launch traced here: 122 us
  Pallas kernels  122 us (99%)
    pallas_call x1, Pallas kernels, turn(): pl.pallas_call(functools.partial(turn_kernel, n, bands, time_len), out_sh...  112 us
    pallas_call x1, Pallas kernels, fdmt(): pl.pallas_call(functools.partial(fdmt_kernel, n), grid=(blocks,), out_sha...  9.99 us

commit v1 on v0

--- a/solution.py
+++ b/solution.py
@@ -12,6 +12,7 @@
 TILE = 8
 BAND = 2**SECTIONS
 LANES = 128
+AT_ONCE = 4
 MESH = pl.DeviceIdType.MESH
 
 epsilon = 1e-05
@@ -106,11 +107,12 @@
     for s in range(SECTIONS):
         target = (buf_a, buf_b)[s % 2]
 
-        def step(p, inner, s=s, source=source, target=target):
-            merge_pair(s, p, source, target, table_row, ident, stage, split)
+        def step(i, inner, s=s, source=source, target=target):
+            for p in range(AT_ONCE):
+                merge_pair(s, i * AT_ONCE + p, source, target, table_row, ident, stage, split)
             return inner
 
-        lax.fori_loop(0, BAND // 2, step, 0)
+        lax.fori_loop(0, BAND // 2 // AT_ONCE, step, 0)
         source = target
 
 
@@ -173,35 +175,47 @@
     ident = eye(LANES)
     groups = table.shape[2] // LANES
     per_group = LANES // BAND
-    group_row = lax.broadcasted_iota(jnp.int32, (groups, LANES), 0)
-    lane = lax.broadcasted_iota(jnp.int32, (groups, LANES), 1)
-    lane_q = lane % (LANES // 2)
+    pairs = SECTIONS * MAXBLK // 2
+
+    def spread_table(s, carry):
+        for c in range(groups):
+            lines[pl.ds(s * (MAXBLK * groups) + c, MAXBLK, stride=groups), :] = table[
+                s, :, c * LANES : (c + 1) * LANES
+            ].astype(jnp.float32)
+        return carry
+
+    lax.fori_loop(0, SECTIONS, spread_table, 0)
+    turned = times_transposed(ident, lines[...].astype(jnp.bfloat16))
+    turned = jnp.concatenate(
+        [
+            jnp.concatenate(
+                [
+                    turned[b * BAND : (b + 1) * BAND, q * 2 * groups : (q + 1) * 2 * groups]
+                    for b in range(per_group)
+                ],
+                axis=1,
+            )
+            for q in range(pairs)
+        ],
+        axis=0,
+    ).astype(jnp.bfloat16)
+    shape = (per_group * 2 * groups, 2 * LANES)
+    index = lax.broadcasted_iota(jnp.int32, shape, 0)
+    lane = lax.broadcasted_iota(jnp.int32, shape, 1)
+    same = (index // groups) % 2 == lane // LANES
+    band = (index % groups) * per_group + index // (2 * groups)
     parts = (
-        ((me // half) * LANES, lane, tab_near),
-        ((flip(me, half) // quarter) * (LANES // 2), lane_q, tab_mid),
-        ((flip(me, half + quarter) // quarter) * (LANES // 2), lane_q, tab_far),
+        ((me // half) * LANES, lane % LANES, tab_near),
+        ((flip(me, half) // quarter) * (LANES // 2), lane % (LANES // 2), tab_mid),
+        ((flip(me, half + quarter) // quarter) * (LANES // 2), lane % (LANES // 2), tab_far),
     )
-
-    def order_table(s, carry):
-        for c in range(groups):
-            lines[pl.ds(c, MAXBLK, stride=groups), :] = table[s, :, c * LANES : (c + 1) * LANES].astype(
-                jnp.float32
-            )
-        for block in range(MAXBLK):
-            part = lines[block * groups : (block + 1) * groups, :].astype(jnp.bfloat16)
-            turned = times_transposed(ident, part).astype(jnp.bfloat16)
-            for start, lanes, target in parts:
-                total = jnp.zeros((BAND, LANES), jnp.float32)
-                for b in range(per_group):
-                    place = (group_row * per_group + b) - start == lanes
-                    place = place.astype(jnp.float32).astype(jnp.bfloat16)
-                    total += jnp.dot(
-                        turned[b * BAND : (b + 1) * BAND], place, preferred_element_type=jnp.float32
-                    )
-                target[block, s] = total.astype(jnp.int32)
-        return carry
-
-    lax.fori_loop(0, SECTIONS, order_table, 0)
+    for start, lanes, target in parts:
+        place = (same & (band - start == lanes)).astype(jnp.float32).astype(jnp.bfloat16)
+        placed = jnp.dot(turned, place, preferred_element_type=jnp.float32).astype(jnp.int32)
+        for q in range(pairs):
+            for i in range(2):
+                s, block = divmod(2 * q + i, MAXBLK)
+                target[block, s] = placed[q * BAND : (q + 1) * BAND, i * LANES : (i + 1) * LANES]
     tab_copy = pltpu.make_async_copy(tab_far, far_table, tab_sem)
     tab_copy.start()
 
@@ -209,11 +223,8 @@
     for k in range(1, half):
         copies[k].wait_recv()
 
-    def fill(d, carry):
+    for d in range(BAND):
         bands_to_lanes(ident, near, d, first)
-        return carry
-
-    lax.fori_loop(0, BAND, fill, 0)
 
     def near_block(block, carry):
         def table_row(s, row):
@@ -229,11 +240,8 @@
     for k in range(half, half + quarter):
         copies[k].wait_recv()
 
-    def fill_q(d, carry):
+    for d in range(BAND):
         bands_to_lanes(ident, mid, d, first_q)
-        return carry
-
-    lax.fori_loop(0, BAND, fill_q, 0)
 
     def mid_block(block, carry):
         def table_row(s, row):
@@ -284,7 +292,7 @@
             pltpu.VMEM((n, BAND, bands, time_len), jnp.bfloat16),
             pltpu.VMEM((n // 2, BAND, bands, time_len), jnp.bfloat16),
             pltpu.VMEM((n // 4, BAND, bands, time_len), jnp.bfloat16),
-            pltpu.VMEM((blocks * groups, LANES), jnp.float32),
+            pltpu.VMEM((sections * blocks * groups, LANES), jnp.float32),
             pltpu.VMEM(ordered, jnp.int32),
             pltpu.VMEM(ordered, jnp.int32),
             pltpu.VMEM(ordered, jnp.int32),
@@ -314,64 +322,122 @@
     )(power, table)
 
 
-def fdmt_kernel(n, count_ref, x_ref, tab_ref, near_ref, mid_ref, o_ref, first, buf_a, buf_b, stage):
-    block = pl.program_id(0)
+def fdmt_kernel(
+    n, count_ref, far_hbm, tab_hbm, near_hbm, mid_hbm, o_hbm,
+    x, tab, zeros, first, buf_a, buf_b, stage, done,
+    in_sem, near_sem, mid_sem, zero_sem, done_sem,
+):
     me = lax.axis_index("chan")
     count = count_ref[lax.axis_index("grp") * n + me]
     half = n // 2
     quarter = n // 4
-    quarter_rows = mid_ref.shape[1]
+    blocks, quarter_rows, _ = mid_hbm.shape
 
     def rows_of(first_quarter, size):
         start = pl.multiple_of(first_quarter * quarter_rows, quarter_rows)
         return pl.ds(start, size * quarter_rows)
 
-    @pl.when(block == 0)
+    loads = [
+        pltpu.make_async_copy(far_hbm, x, in_sem.at[0]),
+        pltpu.make_async_copy(tab_hbm, tab, in_sem.at[1]),
+    ]
+    for load in loads:
+        load.start()
+
+    def near_copy(j):
+        place = o_hbm.at[0, j, rows_of((me // half) * 2, 2)]
+        return pltpu.make_async_copy(near_hbm.at[j], place, near_sem.at[j])
+
+    def mid_copy(j):
+        place = o_hbm.at[0, j, rows_of(flip(me, half) // quarter, 1)]
+        return pltpu.make_async_copy(mid_hbm.at[j], place, mid_sem.at[j])
+
+    def far_copy(j):
+        place = o_hbm.at[0, j, rows_of(flip(me, half + quarter) // quarter, 1)]
+        return pltpu.make_async_copy(done.at[j], place, done_sem.at[j])
+
+    def zero_copy(j):
+        return pltpu.make_async_copy(zeros, o_hbm.at[0, j], zero_sem.at[j])
+
+    for j in range(blocks):
+
+        @pl.when(j < count)
+        def _(j=j):
+            near_copy(j).start()
+            mid_copy(j).start()
+
+    @pl.when(count < blocks)
     def _():
-        ident = eye(x_ref.shape[3])
-        for d in range(BAND):
-            bands_to_lanes(ident, x_ref, d, first)
-
-    @pl.when(block < count)
-    def _():
-        ident = eye(LANES)
-
+        zeros[...] = jnp.zeros_like(zeros)
+
+    for j in range(blocks):
+
+        @pl.when(j >= count)
+        def _(j=j):
+            zero_copy(j).start()
+
+    for load in loads:
+        load.wait()
+    ident = eye(LANES)
+    for d in range(BAND):
+        bands_to_lanes(ident, x, d, first)
+
+    def far_block(j, carry):
         def table_row(s, row):
-            return tab_ref[0, s, pl.ds(row, 1), :]
-
-        o_ref[0, 0, rows_of((me // half) * 2, 2), :] = near_ref[0]
-        o_ref[0, 0, rows_of(flip(me, half) // quarter, 1), :] = mid_ref[0]
+            return tab[j, s, pl.ds(row, 1), :]
+
         source = first
         for s in range(SECTIONS):
             target = (buf_a, buf_b)[s % 2]
             for p in range(BAND // 2):
                 merge_pair(s, p, source, target, table_row, ident, stage, True)
             source = target
-        o_ref[0, 0, rows_of(flip(me, half + quarter) // quarter, 1), :] = stage[...].astype(jnp.bfloat16)
-
-    @pl.when(block >= count)
-    def _():
-        o_ref[...] = jnp.zeros_like(o_ref)
+        done[j] = stage[...].astype(jnp.bfloat16)
+        far_copy(j).start()
+        return carry
+
+    lax.fori_loop(0, count, far_block, 0)
+
+    for j in range(blocks):
+
+        @pl.when(j < count)
+        def _(j=j):
+            near_copy(j).wait()
+            mid_copy(j).wait()
+            far_copy(j).wait()
+
+        @pl.when(j >= count)
+        def _(j=j):
+            zero_copy(j).wait()
 
 
 def fdmt(counts, far, table, near, mid, n):
-    sources, _, bands, time_len = far.shape
+    time_len = far.shape[3]
     blocks, half_rows, _ = near.shape
     rows = 2 * half_rows
+    quarter_rows = half_rows // 2
     wide = pltpu.VMEM((BAND, time_len // TILE // 2, TILE, LANES), jnp.float32)
+    any_spec = pl.BlockSpec(memory_space=pl.ANY)
     return pl.pallas_call(
         functools.partial(fdmt_kernel, n),
-        grid=(blocks,),
         out_shape=jax.ShapeDtypeStruct((1, blocks, rows, time_len), jnp.bfloat16),
-        in_specs=[
-            pl.BlockSpec(memory_space=pltpu.SMEM),
-            pl.BlockSpec(far.shape, lambda j: (0, 0, 0, 0)),
-            pl.BlockSpec((1,) + table.shape[1:], lambda j: (j, 0, 0, 0)),
-            pl.BlockSpec((1, half_rows, time_len), lambda j: (j, 0, 0)),
-            pl.BlockSpec((1, half_rows // 2, time_len), lambda j: (j, 0, 0)),
+        in_specs=[pl.BlockSpec(memory_space=pltpu.SMEM)] + [any_spec] * 4,
+        out_specs=any_spec,
+        scratch_shapes=[
+            pltpu.VMEM(far.shape, far.dtype),
+            pltpu.VMEM(table.shape, table.dtype),
+            pltpu.VMEM((rows, time_len), jnp.bfloat16),
+            wide,
+            wide,
+            wide,
+            pltpu.VMEM((quarter_rows, time_len), jnp.float32),
+            pltpu.VMEM((blocks, quarter_rows, time_len), jnp.bfloat16),
+            pltpu.SemaphoreType.DMA((2,)),
+            pltpu.SemaphoreType.DMA((blocks,)),
+            pltpu.SemaphoreType.DMA((blocks,)),
+            pltpu.SemaphoreType.DMA((blocks,)),
+            pltpu.SemaphoreType.DMA((blocks,)),
         ],
-        out_specs=pl.BlockSpec((1, 1, rows, time_len), lambda j: (0, j, 0, 0)),
-        scratch_shapes=[wide, wide, wide, pltpu.VMEM((half_rows // 2, time_len), jnp.float32)],
         compiler_params=pltpu.CompilerParams(vmem_limit_bytes=58 * 2**20),
         name="fdmt",
     )(counts, far, table, near, mid)

time: 123 us -> 255 us (2.07)
  the two profiles are of different devices: /device:TPU:0 before, /device:TPU:3 now
where the time goes in v1:
time: 255 us; the launch traced here: 254 us
  Pallas kernels  254 us (100%)
    pallas_call x1, Pallas kernels, fdmt(): pl.pallas_call(functools.partial(fdmt_kernel, n), out_shape=jax.ShapeDtyp...  193 us
    pallas_call x1, Pallas kernels, turn(): pl.pallas_call(functools.partial(turn_kernel, n, bands, time_len), out_sh...  61.8 us

profile of v1, /device:TPU:3, one launch (start us, length us, event | category | flops | bytes accessed | tf_op | source)
XLA Modules:
  0.0 254.3 jit_solution(18122687772015322421)
XLA Ops:
  0.0 61.8 %turn.1 = (bf16[4,4096,128]{2,1,0:T(8,128)(2,1)}, bf16[4,2048,128]{2,1,0:T(8,128)(2,1)}, bf16[2,32,32,128]{3,2,1,0:T(8,128)(2,1)}, s32[4,5,32,128]{3,2,1,0:T(8,128)}) custom-call(bf16[8,1024,128]{2,1,0:T(8,128)(2,1)} %power_hbm.1, s32[5,4,8192]{2,1,0:T(4,128)} %bitcast.1), custom_call_target="tpu_custom_call" | custom-call | tf_op jit(solution)/shard_map/turn/pallas_call | solution.py:278
  61.8 192.5 %fdmt.1 = bf16[1,4,8192,128]{3,2,1,0:T(8,128)(2,1)} custom-call(s32[32]{0:T(128)} %count_ref.1, bf16[2,32,32,128]{3,2,1,0:T(8,128)(2,1)} %get-tuple-element.9.far_hbm, s32[4,5,32,128]{3,2,1,0:T(8,128)} %get-tuple-element.10.tab_hbm, bf16[4,4096,128]{2,1,0:T(8,128)(2,1)} %get-tuple-element.11.near_hbm, bf16[4,2048,128]{2,1,0:T(8,128)(2,1)} %get-tuple-element.12.mid_hbm), custom_call_target="tpu_custom_call" | custom-call | tf_op jit(solution)/shard_map/fdmt/pallas_call | solution.py:421

commit v2 on v0

--- a/solution.py
+++ b/solution.py
@@ -12,6 +12,7 @@
 TILE = 8
 BAND = 2**SECTIONS
 LANES = 128
+AT_ONCE = 4
 MESH = pl.DeviceIdType.MESH
 
 epsilon = 1e-05
@@ -106,11 +107,12 @@
     for s in range(SECTIONS):
         target = (buf_a, buf_b)[s % 2]
 
-        def step(p, inner, s=s, source=source, target=target):
-            merge_pair(s, p, source, target, table_row, ident, stage, split)
+        def step(i, inner, s=s, source=source, target=target):
+            for p in range(AT_ONCE):
+                merge_pair(s, i * AT_ONCE + p, source, target, table_row, ident, stage, split)
             return inner
 
-        lax.fori_loop(0, BAND // 2, step, 0)
+        lax.fori_loop(0, BAND // 2 // AT_ONCE, step, 0)
         source = target
 
 
@@ -126,7 +128,7 @@
     grp = lax.axis_index("grp")
     half = n // 2
     quarter = n // 4
-    order = list(range(half, half + quarter)) + list(range(half - 1, -1, -1)) + list(range(half + quarter, n))
+    order = list(range(half - 1, -1, -1)) + list(range(half, n))
 
     loads = {}
     for k in order:
@@ -173,35 +175,47 @@
     ident = eye(LANES)
     groups = table.shape[2] // LANES
     per_group = LANES // BAND
-    group_row = lax.broadcasted_iota(jnp.int32, (groups, LANES), 0)
-    lane = lax.broadcasted_iota(jnp.int32, (groups, LANES), 1)
-    lane_q = lane % (LANES // 2)
+    pairs = SECTIONS * MAXBLK // 2
+
+    def spread_table(s, carry):
+        for c in range(groups):
+            lines[pl.ds(s * (MAXBLK * groups) + c, MAXBLK, stride=groups), :] = table[
+                s, :, c * LANES : (c + 1) * LANES
+            ].astype(jnp.float32)
+        return carry
+
+    lax.fori_loop(0, SECTIONS, spread_table, 0)
+    turned = times_transposed(ident, lines[...].astype(jnp.bfloat16))
+    turned = jnp.concatenate(
+        [
+            jnp.concatenate(
+                [
+                    turned[b * BAND : (b + 1) * BAND, q * 2 * groups : (q + 1) * 2 * groups]
+                    for b in range(per_group)
+                ],
+                axis=1,
+            )
+            for q in range(pairs)
+        ],
+        axis=0,
+    ).astype(jnp.bfloat16)
+    shape = (per_group * 2 * groups, 2 * LANES)
+    index = lax.broadcasted_iota(jnp.int32, shape, 0)
+    lane = lax.broadcasted_iota(jnp.int32, shape, 1)
+    same = (index // groups) % 2 == lane // LANES
+    band = (index % groups) * per_group + index // (2 * groups)
     parts = (
-        ((me // half) * LANES, lane, tab_near),
-        ((flip(me, half) // quarter) * (LANES // 2), lane_q, tab_mid),
-        ((flip(me, half + quarter) // quarter) * (LANES // 2), lane_q, tab_far),
+        ((me // half) * LANES, lane % LANES, tab_near),
+        ((flip(me, half) // quarter) * (LANES // 2), lane % (LANES // 2), tab_mid),
+        ((flip(me, half + quarter) // quarter) * (LANES // 2), lane % (LANES // 2), tab_far),
     )
-
-    def order_table(s, carry):
-        for c in range(groups):
-            lines[pl.ds(c, MAXBLK, stride=groups), :] = table[s, :, c * LANES : (c + 1) * LANES].astype(
-                jnp.float32
-            )
-        for block in range(MAXBLK):
-            part = lines[block * groups : (block + 1) * groups, :].astype(jnp.bfloat16)
-            turned = times_transposed(ident, part).astype(jnp.bfloat16)
-            for start, lanes, target in parts:
-                total = jnp.zeros((BAND, LANES), jnp.float32)
-                for b in range(per_group):
-                    place = (group_row * per_group + b) - start == lanes
-                    place = place.astype(jnp.float32).astype(jnp.bfloat16)
-                    total += jnp.dot(
-                        turned[b * BAND : (b + 1) * BAND], place, preferred_element_type=jnp.float32
-                    )
-                target[block, s] = total.astype(jnp.int32)
-        return carry
-
-    lax.fori_loop(0, SECTIONS, order_table, 0)
+    for start, lanes, target in parts:
+        place = (same & (band - start == lanes)).astype(jnp.float32).astype(jnp.bfloat16)
+        placed = jnp.dot(turned, place, preferred_element_type=jnp.float32).astype(jnp.int32)
+        for q in range(pairs):
+            for i in range(2):
+                s, block = divmod(2 * q + i, MAXBLK)
+                target[block, s] = placed[q * BAND : (q + 1) * BAND, i * LANES : (i + 1) * LANES]
     tab_copy = pltpu.make_async_copy(tab_far, far_table, tab_sem)
     tab_copy.start()
 
@@ -209,11 +223,8 @@
     for k in range(1, half):
         copies[k].wait_recv()
 
-    def fill(d, carry):
+    for d in range(BAND):
         bands_to_lanes(ident, near, d, first)
-        return carry
-
-    lax.fori_loop(0, BAND, fill, 0)
 
     def near_block(block, carry):
         def table_row(s, row):
@@ -229,11 +240,8 @@
     for k in range(half, half + quarter):
         copies[k].wait_recv()
 
-    def fill_q(d, carry):
+    for d in range(BAND):
         bands_to_lanes(ident, mid, d, first_q)
-        return carry
-
-    lax.fori_loop(0, BAND, fill_q, 0)
 
     def mid_block(block, carry):
         def table_row(s, row):
@@ -284,7 +292,7 @@
             pltpu.VMEM((n, BAND, bands, time_len), jnp.bfloat16),
             pltpu.VMEM((n // 2, BAND, bands, time_len), jnp.bfloat16),
             pltpu.VMEM((n // 4, BAND, bands, time_len), jnp.bfloat16),
-            pltpu.VMEM((blocks * groups, LANES), jnp.float32),
+            pltpu.VMEM((sections * blocks * groups, LANES), jnp.float32),
             pltpu.VMEM(ordered, jnp.int32),
             pltpu.VMEM(ordered, jnp.int32),
             pltpu.VMEM(ordered, jnp.int32),

time: 123 us -> 73.4 us (0.60)
  Pallas kernels: 122 us -> 73 us
    pallas_call x1, Pallas kernels: 112 us -> 63 us  [turn(): pl.pallas_call(functools.partial(turn_kernel, n, bands, time_len), out_sh...]
where the time goes in v2:
time: 73.4 us; the launch traced here: 73 us
  Pallas kernels  73 us (99%)
    pallas_call x1, Pallas kernels, turn(): pl.pallas_call(functools.partial(turn_kernel, n, bands, time_len), out_sh...  63 us
    pallas_call x1, Pallas kernels, fdmt(): pl.pallas_call(functools.partial(fdmt_kernel, n), grid=(blocks,), out_sha...  9.99 us

profile of v2, /device:TPU:0, one launch (start us, length us, event | category | flops | bytes accessed | tf_op | source)
XLA Modules:
  0.0 73.0 jit_solution(1463694574053766304)
XLA Ops:
  0.0 63.0 %turn.1 = (bf16[4,4096,128]{2,1,0:T(8,128)(2,1)}, bf16[4,2048,128]{2,1,0:T(8,128)(2,1)}, bf16[2,32,32,128]{3,2,1,0:T(8,128)(2,1)}, s32[4,5,32,128]{3,2,1,0:T(8,128)}) custom-call(bf16[8,1024,128]{2,1,0:T(8,128)(2,1)} %power_hbm.1, s32[5,4,8192]{2,1,0:T(4,128)} %bitcast.1), custom_call_target="tpu_custom_call" | custom-call | tf_op jit(solution)/shard_map/turn/pallas_call | solution.py:278
  63.0 10.0 %fdmt.1 = bf16[1,4,8192,128]{3,2,1,0:T(8,128)(2,1)} custom-call(s32[32]{0:T(128)} %count_ref.1, bf16[2,32,32,128]{3,2,1,0:T(8,128)(2,1)} %get-tuple-element.9.x_ref, s32[4,5,32,128]{3,2,1,0:T(8,128)} %get-tuple-element.10.tab_ref, bf16[4,4096,128]{2,1,0:T(8,128)(2,1)} %get-tuple-element.11.near_ref, bf16[4,2048,128]{2,1,0:T(8,128)(2,1)} %get-tuple-element.12.mid_ref), custom_call_target="tpu_custom_call" | custom-call | tf_op jit(solution)/shard_map/fdmt/pallas_call | solution.py:370
